TPU v7x, 32 devices: a whole 2x2x4 slice. The times are simulated.
32 devices in a mesh: dp: 4 (over x, core), term: 8 (over z, y).
Axes of the slice: x: 2, y: 2, z: 4, core: 2. Of those that a mesh axis runs over, the one named last changes fastest.
Arguments:
- inputs: bfloat16 [1024, 8192], P('dp'), may hold values from -6 to 6
- cotangent: bfloat16 [1024, 8192], P('dp', 'term'), may hold values from -6 to 6
- logits: float32 [1024, 256], P('dp'), may hold values from -20 to 320
- in_factor: bfloat16 [8192, 2048], P(None, 'term'), may hold values from -0.09375 to 0.09375
- out_factor: bfloat16 [8192, 2048], P(None, 'term'), may hold values from -0.0625 to 0.0625
- expert_factor: bfloat16 [256, 2048], P(None, 'term'), may hold values from -3 to 3
Outputs:
- grad_inputs: bfloat16 [1024, 8192], P('dp', 'term')
- grad_logits: float32 [1024, 256], P('dp', 'term')
- grad_in_factor: float32 [8192, 2048], P('dp', 'term')
- grad_out_factor: float32 [8192, 2048], P('dp', 'term')
- grad_expert_factor: float32 [256, 2048], P('dp', 'term')
All inputs are finite; a program needn't handle non-finite values.
Results may differ from a plain program's by a relative error of at most 0.028.
Values may be sent and summed in bfloat16 or wider, within the bound.
A program may use at most 128 MiB of HBM per device.

v0:
```python
import math
import jax
import jax.numpy as jnp
from jax import lax
from jax.sharding import PartitionSpec as P


def per_device(inputs, cotangent, logits, in_factor, out_factor, expert_factor):
    fl = jnp.float32
    n_term = lax.axis_size("term")
    n_data = lax.axis_size("dp")
    gates = jax.nn.softmax(logits, axis=-1)
    gates_bf = gates.astype(jnp.bfloat16)
    proj_in = jnp.dot(inputs, in_factor, preferred_element_type=fl)
    proj_exp = jnp.dot(gates_bf, expert_factor, preferred_element_type=fl)
    hidden = (proj_in * proj_exp).astype(jnp.bfloat16)
    full_cotan = lax.all_gather(cotangent, "term", axis=1, tiled=True)
    grad_hid = jnp.dot(full_cotan, out_factor, preferred_element_type=fl)
    grad_pin = (grad_hid * proj_exp).astype(jnp.bfloat16)
    grad_pexp = (grad_hid * proj_in).astype(jnp.bfloat16)
    row_total = lax.psum(jnp.sum(grad_hid * proj_in * proj_exp, axis=1, keepdims=True), "term")
    contract_last = (((1,), (1,)), ((), ()))
    part_x = lax.dot_general(grad_pin, in_factor, contract_last, preferred_element_type=fl)
    part_g = lax.dot_general(grad_pexp, expert_factor, contract_last, preferred_element_type=fl)
    sum_x, grad_gate = (
        lax.psum_scatter(
            part_x.astype(jnp.bfloat16), "term", scatter_dimension=1, tiled=True
        ).astype(jnp.float32),
        lax.psum_scatter(
            part_g.astype(jnp.bfloat16), "term", scatter_dimension=1, tiled=True
        ).astype(jnp.float32),
    )
    grad_inputs = sum_x.astype(jnp.bfloat16)
    exp_local = logits.shape[1] // n_term
    gates_local = lax.dynamic_slice_in_dim(gates, lax.axis_index("term") * exp_local, exp_local, 1)
    grad_logits = gates_local * (grad_gate - row_total)
    scale = 1.0 / math.sqrt(inputs.shape[0] * n_data)
    contract_first = (((0,), (0,)), ((), ()))
    part_in = lax.dot_general(inputs, grad_pin, contract_first, preferred_element_type=fl) * scale
    part_out = (
        lax.dot_general(full_cotan, hidden, contract_first, preferred_element_type=fl) * scale
    )
    part_exp = (
        lax.dot_general(gates_bf, grad_pexp, contract_first, preferred_element_type=fl) * scale
    )
    grad_in, grad_out, grad_exp = (
        lax.psum_scatter(
            part_in.astype(jnp.bfloat16), "dp", scatter_dimension=0, tiled=True
        ).astype(jnp.float32),
        lax.psum_scatter(
            part_out.astype(jnp.bfloat16), "dp", scatter_dimension=0, tiled=True
        ).astype(jnp.float32),
        lax.psum_scatter(
            part_exp.astype(jnp.bfloat16), "dp", scatter_dimension=0, tiled=True
        ).astype(jnp.float32),
    )
    return (grad_inputs, grad_logits, grad_in, grad_out, grad_exp)


def solution(mesh):
    return jax.shard_map(
        per_device,
        mesh=mesh,
        in_specs=(
            P("dp", None),
            P("dp", "term"),
            P("dp", None),
            P(None, "term"),
            P(None, "term"),
            P(None, "term"),
        ),
        out_specs=(
            P("dp", "term"),
            P("dp", "term"),
            P("dp", "term"),
            P("dp", "term"),
            P("dp", "term"),
        ),
        check_vma=False,
    )
```

profile of v0, /device:TPU:0, one launch (start us, length us, event | category | flops | bytes accessed | tf_op | source)
XLA Modules:
  0.0 368.6 jit_solution(12951424411813804137)
XLA Ops:
  7.2 0.0 copy-start
  7.2 0.0 all-gather.2.cloned.1.call-start
  7.2 0.7 all-gather.2.cloned.1.call-update
  7.9 0.0 reduce-scatter.14.cloned.1.call-start
  8.0 1.1 copy.11
  9.1 1.1 reduce_max.9
  10.1 0.1 fusion.6
  10.2 5.2 %fusion.11 = f32[256,256]{0,1:T(8,128)S(1)} fusion(bf16[256,8192]{1,0:T(8,128)(2,1)} %param.6, bf16[8192,256]{1,0:T(8,128)(2,1)} %param.9), kind=kOutput, calls=%fused_computation.22 | convolution fusion | flops 1073741824 | bytes 8650752 | tf_op jit(solution)/shard_map/dot_general | solution.py:14
  15.5 70.9 %all-gather.2.cloned.1.call-done = bf16[256,8192]{1,0:T(8,128)(2,1)} async-done(((bf16[256,1024]{1,0:T(8,128)(2,1)}), bf16[256,8192]{1,0:T(8,128)(2,1)}) %all-gather.2.cloned.1.call-update) | async-done | bytes 4194320 | tf_op jit(solution)/shard_map/all_gather | solution.py:17
  86.3 5.2 %fusion.10 = f32[256,256]{0,1:T(8,128)S(1)} fusion(bf16[256,8192]{1,0:T(8,128)(2,1)} %all-gather.2.cloned.1.call-done, bf16[8192,256]{1,0:T(8,128)(2,1)} %param.10), kind=kOutput, calls=%fused_computation.21 | convolution fusion | flops 1073741824 | bytes 8650752 | tf_op jit(solution)/shard_map/dot_general | solution.py:18
  91.5 0.0 copy-done
  91.5 0.3 multiply_reduce_fusion
  91.8 0.9 fusion.4
  92.7 0.0 reduce-scatter.14.cloned.1.call-update
  92.7 0.0 reduce-scatter.8.cloned.1.call-start
  92.7 0.8 convolution_convert_fusion.1
  93.6 0.0 reduce-scatter.8.cloned.1.call-update
  93.6 0.0 reduce-scatter.12.cloned.1.call-start
  93.7 5.4 %fusion.2 = bf16[8192,256]{0,1:T(8,128)(2,1)} fusion(bf16[256,8192]{1,0:T(8,128)(2,1)} %all-gather.2.cloned.1.call-done, f32[256,256]{0,1:T(8,128)S(1)} %fusion.11, f32[256,256]{0,1:T(8,128)S(1)} %get-tuple-element.13), kind=kOutput, calls=%fused_computation.5 | convolution fusion | flops 1078067200 | bytes 8912896 | tf_op jit(solution)/shard_map/dot_general | solution.py:41
  99.1 0.0 reduce-scatter.12.cloned.1.call-update
  99.1 0.0 reduce-scatter.10.cloned.1.call-start
  99.1 5.4 %fusion.3 = bf16[8192,256]{0,1:T(8,128)(2,1)} fusion(bf16[256,256]{0,1:T(8,128)(2,1)S(1)} %get-tuple-element.12, bf16[256,8192]{1,0:T(8,128)(2,1)} %param.6), kind=kOutput, calls=%fused_computation.6 | convolution fusion | flops 1077936128 | bytes 8519680 | tf_op jit(solution)/shard_map/dot_general | solution.py:39
  104.6 0.0 reduce-scatter.10.cloned.1.call-update
  104.6 0.0 reduce-scatter.6.cloned.1.call-start
  104.6 5.5 %convolution_convert_fusion = bf16[256,8192]{1,0:T(8,128)(2,1)} fusion(bf16[256,256]{0,1:T(8,128)(2,1)S(1)} %get-tuple-element.12, bf16[8192,256]{1,0:T(8,128)(2,1)} %param.9), kind=kOutput, calls=%fused_computation.2 | convolution fusion | flops 1075838976 | bytes 8519680 | tf_op jit(solution)/shard_map/dot_general | solution.py:23
  110.1 0.0 reduce-scatter.6.cloned.1.call-update
  110.2 18.7 %psum.7 = f32[256]{0:T(256)S(1)} all-reduce(f32[256]{0:T(256)S(1)} %get-tuple-element.10), channel_id=1, replica_groups=mesh['dp'=4,'term'=8] {'term'}, use_global_device_ids=true, to_apply=%region_5.0 | all-reduce | flops 256 | bytes 2048 | tf_op jit(solution)/shard_map/psum | solution.py:21
  128.9 0.0 reduce-scatter.14.cloned.1.call-done
  128.9 1.4 convert_element_type.61
  130.3 45.6 %reduce-scatter.8.cloned.1.call-done = bf16[256,32]{0,1:T(8,128)(2,1)} async-done(((bf16[256,256]{0,1:T(8,128)(2,1)}), bf16[256,32]{0,1:T(8,128)(2,1)}) %reduce-scatter.8.cloned.1.call-update) | async-done | bytes 16400 | tf_op jit(solution)/shard_map/reduce_scatter | solution.py:29
  175.9 1.3 subtract_multiply_fusion
  177.2 44.8 %reduce-scatter.12.cloned.1.call-done = bf16[2048,256]{0,1:T(8,128)(2,1)} async-done(((bf16[8192,256]{0,1:T(8,128)(2,1)}), bf16[2048,256]{0,1:T(8,128)(2,1)}) %reduce-scatter.12.cloned.1.call-update) | async-done | bytes 1048592 | tf_op jit(solution)/shard_map/reduce_scatter | solution.py:50
  222.0 2.6 copy.13
  224.6 44.4 %reduce-scatter.10.cloned.1.call-done = bf16[2048,256]{0,1:T(8,128)(2,1)} async-done(((bf16[8192,256]{0,1:T(8,128)(2,1)}), bf16[2048,256]{0,1:T(8,128)(2,1)}) %reduce-scatter.10.cloned.1.call-update) | async-done | bytes 1048592 | tf_op jit(solution)/shard_map/reduce_scatter | solution.py:47
  268.9 2.6 copy.12
  271.5 90.3 %reduce-scatter.6.cloned.1.call-done = bf16[256,1024]{1,0:T(8,128)(2,1)} async-done(((bf16[256,8192]{1,0:T(8,128)(2,1)}), bf16[256,1024]{1,0:T(8,128)(2,1)}) %reduce-scatter.6.cloned.1.call-update) | async-done | bytes 524304 | tf_op jit(solution)/shard_map/reduce_scatter | solution.py:26
  (1 shorter events, 0.0 us)
Async XLA Ops:
  7.2 84.4 %copy-start = (bf16[256,256]{1,0:T(8,128)(2,1)S(1)}, bf16[256,256]{1,0:T(8,128)(2,1)}, u32[]{:S(2)}) copy-start(bf16[256,256]{1,0:T(8,128)(2,1)} %param.11) | copy-start | bytes 393220
  7.2 79.1 %all-gather.2.cloned.1.call-start = ((), (), s32[]{:S(2)}) async-start(), calls=%async_computation.5 | async-start | bytes 4718592 | tf_op jit(solution)/shard_map/all_gather | solution.py:17
  7.9 121.0 %reduce-scatter.14.cloned.1.call-start = ((), (), s32[]{:S(2)}) async-start(), calls=%async_computation.10 | async-start | bytes 163840 | tf_op jit(solution)/shard_map/reduce_scatter | solution.py:53
  92.7 83.2 %reduce-scatter.8.cloned.1.call-start = ((), (), s32[]{:S(2)}) async-start(), calls=%async_computation.7 | async-start | bytes 147456 | tf_op jit(solution)/shard_map/reduce_scatter | solution.py:29
  93.6 128.4 %reduce-scatter.12.cloned.1.call-start = ((), (), s32[]{:S(2)}) async-start(), calls=%async_computation.9 | async-start | bytes 5242880 | tf_op jit(solution)/shard_map/reduce_scatter | solution.py:50
  99.1 169.8 %reduce-scatter.10.cloned.1.call-start = ((), (), s32[]{:S(2)}) async-start(), calls=%async_computation.8 | async-start | bytes 5242880 | tf_op jit(solution)/shard_map/reduce_scatter | solution.py:47
  104.6 257.2 %reduce-scatter.6.cloned.1.call-start = ((), (), s32[]{:S(2)}) async-start(), calls=%async_computation.6 | async-start | bytes 4718592 | tf_op jit(solution)/shard_map/reduce_scatter | solution.py:26
Sparse Core Ops, SparseCore 0:
  10.2 76.0 all-gather.1
  92.8 17.8 reduce-scatter.13
  114.9 60.8 reduce-scatter.7
  178.4 43.5 reduce-scatter.11
  224.4 44.4 reduce-scatter.9
  273.4 88.2 reduce-scatter.5
where the time goes:
time: 369 us
  waiting for transfers between devices  297 us (80%)
  matrix products  28.7 us (8%)
  blocking collectives  18.7 us (5%)
  between operations  14.2 us (4%)
  local copies, waits for them, and re-layouts  6.21 us (2%)
  other arithmetic  3.91 us (1%)
    reduce_scatter x1, waiting for transfers between devices, per_device(): lax.psum_scatter(part_x.astype(jnp.bfloat16), 'term', scatter_dimension=1...  90.3 us
    all_gather x1, waiting for transfers between devices, per_device(): full_cotan = lax.all_gather(cotangent, 'term', axis=1, tiled=True)  70.9 us
    reduce_scatter x1, waiting for transfers between devices, per_device(): lax.psum_scatter(part_g.astype(jnp.bfloat16), 'term', scatter_dimension=1...  45.6 us
    reduce_scatter x1, waiting for transfers between devices, per_device(): lax.psum_scatter(part_out.astype(jnp.bfloat16), 'dp', scatter_dimension=0...  44.8 us
    reduce_scatter x1, waiting for transfers between devices, per_device(): lax.psum_scatter(part_in.astype(jnp.bfloat16), 'dp', scatter_dimension=0,...  44.4 us
    psum x1, blocking collectives, per_device(): lax.psum(jnp.sum(grad_hid * proj_in * proj_exp, axis=1, keepdims=True), '...  18.7 us
  transfers between devices with their start and end apart: 6, of which 5 were waited for; matrix products, arithmetic and copies ran while one was open for 9% of the time, Pallas kernels for 0%

commit v1 on v0

--- a/solution.py
+++ b/solution.py
@@ -1,8 +1,16 @@
+import functools
 import math
 import jax
 import jax.numpy as jnp
 from jax import lax
 from jax.sharding import PartitionSpec as P
+
+
+def obtain_space(array_in, a_name):
+    return lax.all_gather(array_in, axis_name=a_name).sum(axis=0)
+
+
+link_local_data = functools.partial(obtain_space, a_name="term")
 
 
 def per_device(inputs, cotangent, logits, in_factor, out_factor, expert_factor):
@@ -18,7 +26,7 @@
     grad_hid = jnp.dot(full_cotan, out_factor, preferred_element_type=fl)
     grad_pin = (grad_hid * proj_exp).astype(jnp.bfloat16)
     grad_pexp = (grad_hid * proj_in).astype(jnp.bfloat16)
-    row_total = lax.psum(jnp.sum(grad_hid * proj_in * proj_exp, axis=1, keepdims=True), "term")
+    row_total = link_local_data(jnp.sum(grad_hid * proj_in * proj_exp, axis=1, keepdims=True))
     contract_last = (((1,), (1,)), ((), ()))
     part_x = lax.dot_general(grad_pin, in_factor, contract_last, preferred_element_type=fl)
     part_g = lax.dot_general(grad_pexp, expert_factor, contract_last, preferred_element_type=fl)

time: 369 us -> 369 us (level)
    psum x1 -> x0, blocking collectives: 18.7 us -> none  [per_device(): lax.psum(jnp.sum(grad_hid * proj_in * proj_exp, axis=1, keepdims=True), '...]
    all_gather x0 -> x1, blocking collectives: none -> 17.9 us  [obtain_space(): return lax.all_gather(array_in, axis_name=a_name).sum(axis=0)]
where the time goes in v1:
time: 369 us
  waiting for transfers between devices  297 us (80%)
  matrix products  28.7 us (8%)
  blocking collectives  17.9 us (5%)
  between operations  14.2 us (4%)
  local copies, waits for them, and re-layouts  6.21 us (2%)
  other arithmetic  3.94 us (1%)
    reduce_scatter x1, waiting for transfers between devices, per_device(): lax.psum_scatter(part_x.astype(jnp.bfloat16), 'term', scatter_dimension=1...  90.3 us
    all_gather x1, waiting for transfers between devices, per_device(): full_cotan = lax.all_gather(cotangent, 'term', axis=1, tiled=True)  70.9 us
    reduce_scatter x1, waiting for transfers between devices, per_device(): lax.psum_scatter(part_g.astype(jnp.bfloat16), 'term', scatter_dimension=1...  46.4 us
    reduce_scatter x1, waiting for transfers between devices, per_device(): lax.psum_scatter(part_out.astype(jnp.bfloat16), 'dp', scatter_dimension=0...  44.8 us
    reduce_scatter x1, waiting for transfers between devices, per_device(): lax.psum_scatter(part_in.astype(jnp.bfloat16), 'dp', scatter_dimension=0,...  44.4 us
    all_gather x1, blocking collectives, obtain_space(): return lax.all_gather(array_in, axis_name=a_name).sum(axis=0)  17.9 us
  transfers between devices with their start and end apart: 6, of which 5 were waited for; matrix products, arithmetic and copies ran while one was open for 9% of the time, Pallas kernels for 0%

profile of v1, /device:TPU:0, one launch (start us, length us, event | category | flops | bytes accessed | tf_op | source)
XLA Modules:
  0.0 368.6 jit_solution(2575955475367786367)
XLA Ops:
  7.2 0.0 copy-start
  7.2 0.0 all-gather.4.cloned.1.call-start
  7.2 0.7 all-gather.4.cloned.1.call-update
  7.9 0.0 reduce-scatter.14.cloned.1.call-start
  8.0 1.1 copy.14
  9.1 1.1 reduce_max.9
  10.1 0.1 fusion.6
  10.2 5.2 %fusion.11 = f32[256,256]{0,1:T(8,128)S(1)} fusion(bf16[256,8192]{1,0:T(8,128)(2,1)} %param.6, bf16[8192,256]{1,0:T(8,128)(2,1)} %param.9), kind=kOutput, calls=%fused_computation.22 | convolution fusion | flops 1073741824 | bytes 8650752 | tf_op jit(solution)/shard_map/dot_general | solution.py:22
  15.5 70.9 %all-gather.4.cloned.1.call-done = bf16[256,8192]{1,0:T(8,128)(2,1)} async-done(((bf16[256,1024]{1,0:T(8,128)(2,1)}), bf16[256,8192]{1,0:T(8,128)(2,1)}) %all-gather.4.cloned.1.call-update) | async-done | bytes 4194320 | tf_op jit(solution)/shard_map/all_gather | solution.py:25
  86.3 5.2 %fusion.10 = f32[256,256]{0,1:T(8,128)S(1)} fusion(bf16[256,8192]{1,0:T(8,128)(2,1)} %all-gather.4.cloned.1.call-done, bf16[8192,256]{1,0:T(8,128)(2,1)} %param.10), kind=kOutput, calls=%fused_computation.21 | convolution fusion | flops 1073741824 | bytes 8650752 | tf_op jit(solution)/shard_map/dot_general | solution.py:26
  91.5 0.0 copy-done
  91.5 0.3 multiply_reduce_fusion
  91.8 0.9 fusion.4
  92.7 0.0 reduce-scatter.14.cloned.1.call-update
  92.7 0.0 reduce-scatter.8.cloned.1.call-start
  92.7 0.8 convolution_convert_fusion.1
  93.6 0.0 reduce-scatter.8.cloned.1.call-update
  93.6 0.0 reduce-scatter.12.cloned.1.call-start
  93.7 5.4 %fusion.2 = bf16[8192,256]{0,1:T(8,128)(2,1)} fusion(bf16[256,8192]{1,0:T(8,128)(2,1)} %all-gather.4.cloned.1.call-done, f32[256,256]{0,1:T(8,128)S(1)} %fusion.11, f32[256,256]{0,1:T(8,128)S(1)} %get-tuple-element.18), kind=kOutput, calls=%fused_computation.5 | convolution fusion | flops 1078067200 | bytes 8912896 | tf_op jit(solution)/shard_map/dot_general | solution.py:49
  99.1 0.0 reduce-scatter.12.cloned.1.call-update
  99.1 0.0 reduce-scatter.10.cloned.1.call-start
  99.1 5.4 %fusion.3 = bf16[8192,256]{0,1:T(8,128)(2,1)} fusion(bf16[256,256]{0,1:T(8,128)(2,1)S(1)} %get-tuple-element.17, bf16[256,8192]{1,0:T(8,128)(2,1)} %param.6), kind=kOutput, calls=%fused_computation.6 | convolution fusion | flops 1077936128 | bytes 8519680 | tf_op jit(solution)/shard_map/dot_general | solution.py:47
  104.6 0.0 reduce-scatter.10.cloned.1.call-update
  104.6 0.0 reduce-scatter.6.cloned.1.call-start
  104.6 5.5 %convolution_convert_fusion = bf16[256,8192]{1,0:T(8,128)(2,1)} fusion(bf16[256,256]{0,1:T(8,128)(2,1)S(1)} %get-tuple-element.17, bf16[8192,256]{1,0:T(8,128)(2,1)} %param.9), kind=kOutput, calls=%fused_computation.2 | convolution fusion | flops 1075838976 | bytes 8519680 | tf_op jit(solution)/shard_map/dot_general | solution.py:31
  110.1 0.0 reduce-scatter.6.cloned.1.call-update
  110.2 17.9 %all-gather.1 = f32[8,1,256]{2,1,0:T(1,128)S(1)} all-gather(f32[1,1,256]{2,1,0:T(1,128)S(1)} %bitcast.18), channel_id=2, replica_groups=mesh['dp'=4,'term'=8] {'term'}, dimensions={0}, use_global_device_ids=true | all-gather | bytes 9216 | tf_op jit(solution)/shard_map/all_gather | solution.py:10
  128.0 0.0 reduce-scatter.14.cloned.1.call-done
  128.1 1.4 convert_element_type.61
  129.5 46.4 %reduce-scatter.8.cloned.1.call-done = bf16[256,32]{0,1:T(8,128)(2,1)} async-done(((bf16[256,256]{0,1:T(8,128)(2,1)}), bf16[256,32]{0,1:T(8,128)(2,1)}) %reduce-scatter.8.cloned.1.call-update) | async-done | bytes 16400 | tf_op jit(solution)/shard_map/reduce_scatter | solution.py:37
  175.9 1.3 subtract_multiply_fusion
  177.2 44.8 %reduce-scatter.12.cloned.1.call-done = bf16[2048,256]{0,1:T(8,128)(2,1)} async-done(((bf16[8192,256]{0,1:T(8,128)(2,1)}), bf16[2048,256]{0,1:T(8,128)(2,1)}) %reduce-scatter.12.cloned.1.call-update) | async-done | bytes 1048592 | tf_op jit(solution)/shard_map/reduce_scatter | solution.py:58
  222.0 2.6 copy.16
  224.6 44.4 %reduce-scatter.10.cloned.1.call-done = bf16[2048,256]{0,1:T(8,128)(2,1)} async-done(((bf16[8192,256]{0,1:T(8,128)(2,1)}), bf16[2048,256]{0,1:T(8,128)(2,1)}) %reduce-scatter.10.cloned.1.call-update) | async-done | bytes 1048592 | tf_op jit(solution)/shard_map/reduce_scatter | solution.py:55
  268.9 2.6 copy.15
  271.5 90.3 %reduce-scatter.6.cloned.1.call-done = bf16[256,1024]{1,0:T(8,128)(2,1)} async-done(((bf16[256,8192]{1,0:T(8,128)(2,1)}), bf16[256,1024]{1,0:T(8,128)(2,1)}) %reduce-scatter.6.cloned.1.call-update) | async-done | bytes 524304 | tf_op jit(solution)/shard_map/reduce_scatter | solution.py:34
  (2 shorter events, 0.1 us)
Async XLA Ops:
  7.2 84.4 %copy-start = (bf16[256,256]{1,0:T(8,128)(2,1)S(1)}, bf16[256,256]{1,0:T(8,128)(2,1)}, u32[]{:S(2)}) copy-start(bf16[256,256]{1,0:T(8,128)(2,1)} %param.11) | copy-start | bytes 393220
  7.2 79.1 %all-gather.4.cloned.1.call-start = ((), (), s32[]{:S(2)}) async-start(), calls=%async_computation.5 | async-start | bytes 4718592 | tf_op jit(solution)/shard_map/all_gather | solution.py:25
  7.9 120.1 %reduce-scatter.14.cloned.1.call-start = ((), (), s32[]{:S(2)}) async-start(), calls=%async_computation.10 | async-start | bytes 163840 | tf_op jit(solution)/shard_map/reduce_scatter | solution.py:61
  92.7 83.2 %reduce-scatter.8.cloned.1.call-start = ((), (), s32[]{:S(2)}) async-start(), calls=%async_computation.7 | async-start | bytes 147456 | tf_op jit(solution)/shard_map/reduce_scatter | solution.py:37
  93.6 128.4 %reduce-scatter.12.cloned.1.call-start = ((), (), s32[]{:S(2)}) async-start(), calls=%async_computation.9 | async-start | bytes 5242880 | tf_op jit(solution)/shard_map/reduce_scatter | solution.py:58
  99.1 169.8 %reduce-scatter.10.cloned.1.call-start = ((), (), s32[]{:S(2)}) async-start(), calls=%async_computation.8 | async-start | bytes 5242880 | tf_op jit(solution)/shard_map/reduce_scatter | solution.py:55
  104.6 257.2 %reduce-scatter.6.cloned.1.call-start = ((), (), s32[]{:S(2)}) async-start(), calls=%async_computation.6 | async-start | bytes 4718592 | tf_op jit(solution)/shard_map/reduce_scatter | solution.py:34
Sparse Core Ops, SparseCore 0:
  10.2 76.0 all-gather.3
  92.8 17.8 reduce-scatter.13
  114.9 60.8 reduce-scatter.7
  178.4 43.5 reduce-scatter.11
  224.4 44.4 reduce-scatter.9
  273.4 88.2 reduce-scatter.5
